TPU v7x, 32 devices: a whole 2x2x4 slice. The times are simulated.
32 devices in a mesh: req: 8 (over z, y), hid: 4 (over x, core).
Axes of the slice: x: 2, y: 2, z: 4, core: 2. Of those that a mesh axis runs over, the one named last changes fastest.
Arguments:
- hidden_in: bfloat16 [8, 512, 1536], P('req', 'hid'), may hold values from -6 to 6
- queries: bfloat16 [8, 512, 1536], P('req', 'hid'), may hold values from -4 to 4
- cache_keys: bfloat16 [8, 4096, 256], P('req', 'hid'), may hold values from -6 to 6
- cache_values: bfloat16 [8, 4096, 256], P('req', 'hid'), may hold values from -6 to 6
- lengths: int32 [8], P('req'), may hold values from 256 to 4096, as said below
- routes: int32 [8, 512, 4], P('req'), may hold values from 0 to 7, all different within a row; in each aligned block of 128 rows (0 to 127, 128 to 255, ..., all dimensions but the last counted through in order) at most 128 rows name the same one
- attn_gain: float32 [1536], replicated, may hold values from 0.25 to 1.75
- key_proj: bfloat16 [1536, 256], replicated, may hold values from -0.15625 to 0.15625
- value_proj: bfloat16 [1536, 256], replicated, may hold values from -0.15625 to 0.15625
- out_proj: bfloat16 [1536, 1536], replicated, may hold values from -0.15625 to 0.15625
- moe_gain: float32 [1536], replicated, may hold values from 0.25 to 1.75
- router: bfloat16 [1536, 8], replicated, may hold values from -0.3125 to 0.3125
- gate_up: bfloat16 [8, 2, 1536, 768], P('req', None, None, 'hid'), may hold values from -0.15625 to 0.15625
- down_proj: bfloat16 [8, 768, 1536], P('req', 'hid'), may hold values from -0.21875 to 0.21875
Outputs:
- layer_out: bfloat16 [8, 512, 1536], P('req', 'hid')
- new_keys: bfloat16 [8, 512, 256], P('req', 'hid')
- new_values: bfloat16 [8, 512, 256], P('req', 'hid')
Inputs may be any that keep to these rules, and one draw needn't show every extreme that they name: `routes`: each row names 4 different experts; within each aligned block of 128 tokens (the tokens of one device) no expert is named by more than 128 tokens, and in some block one expert is named by exactly 128. `lengths`: some request holds exactly 4096 cached positions and some other exactly 256.
All inputs are finite; a program needn't handle non-finite values.
Results may differ from a plain program's by a relative error of at most 0.015.
Values may be sent and summed in bfloat16 or wider, within the bound.
A program may use at most 128 MiB of HBM per device.

v0:
```python
import jax
import jax.numpy as jnp
from jax import lax
from jax.sharding import PartitionSpec as P

QH = 12
KVH = 2
HD = 128


EPS = 1e-06
MASKED_SCORE = -1e30
KEY_BLOCK = 512


def normalize(row_data, gain_vector):
    row_data = row_data.astype(jnp.float32)
    return (
        row_data
        * lax.rsqrt(jnp.mean(row_data * row_data, axis=-1, keepdims=True) + EPS)
        * gain_vector
    )


def absorb(state_now, grouped, key_rows, value_rows, visible):
    row_max, totals, accumulated = state_now
    scores = jnp.einsum(
        "tgsd,kgd->gstk", grouped, key_rows.reshape(-1, KVH, HD), preferred_element_type=jnp.float32
    ) * HD ** (-0.5)
    scores = jnp.where(visible, scores, MASKED_SCORE)
    new_max = jnp.maximum(row_max, jnp.max(scores, axis=-1))
    weights = jnp.where(visible, jnp.exp(scores - new_max[..., None]), 0.0)
    rescale = jnp.exp(row_max - new_max)
    totals = totals * rescale + jnp.sum(weights, axis=-1)
    accumulated = accumulated * rescale[..., None] + jnp.einsum(
        "gstk,kgd->gstd",
        weights.astype(jnp.bfloat16),
        value_rows.reshape(-1, KVH, HD),
        preferred_element_type=jnp.float32,
    )
    return (new_max, totals, accumulated)


def cache_block(state_now, grouped, key_rows, value_rows, first_pos, length):
    positions = first_pos + jnp.arange(key_rows.shape[0], dtype=jnp.int32)
    visible = (positions < length)[None, :]
    return lax.cond(
        first_pos < length,
        lambda current: absorb(current, grouped, key_rows, value_rows, visible),
        lambda current: current,
        state_now,
    )


def span_block(state_now, grouped, key_rows, value_rows, first_pos, query_pos):
    positions = first_pos + jnp.arange(key_rows.shape[0], dtype=jnp.int32)
    visible = positions[None, :] <= query_pos[:, None]
    return lax.cond(
        first_pos <= query_pos[-1],
        lambda current: absorb(current, grouped, key_rows, value_rows, visible),
        lambda current: current,
        state_now,
    )


def block_size(extent):
    return max(min(KEY_BLOCK, extent), extent // 8)


def empty_state(query_count):
    group_size = QH // KVH
    return (
        jnp.full((KVH, group_size, query_count), MASKED_SCORE, jnp.float32),
        jnp.zeros((KVH, group_size, query_count), jnp.float32),
        jnp.zeros((KVH, group_size, query_count, HD), jnp.float32),
    )


def expert_activation(row_data, gate_weights):
    gate_out = jnp.dot(row_data, gate_weights[0], preferred_element_type=jnp.float32)
    up_out = jnp.dot(row_data, gate_weights[1], preferred_element_type=jnp.float32)
    return (jnp.maximum(gate_out, 0.0) * up_out).astype(jnp.bfloat16)


def body(
    hidden_in,
    queries,
    cache_keys,
    cache_values,
    lengths,
    routes,
    attn_gain,
    key_proj,
    value_proj,
    out_proj,
    moe_gain,
    router,
    gate_up,
    down_proj,
):
    own_count = hidden_in.shape[1]
    model_width = hidden_in.shape[2]
    hid_index = lax.axis_index("hid")
    hid_count = lax.axis_size("hid")
    group_size = QH // KVH
    normed = normalize(hidden_in[0], attn_gain).astype(jnp.bfloat16)
    new_keys = jnp.dot(normed, key_proj, preferred_element_type=jnp.float32).astype(jnp.bfloat16)[
        None
    ]
    new_values = jnp.dot(normed, value_proj, preferred_element_type=jnp.float32).astype(
        jnp.bfloat16
    )[None]
    length = lengths[0]
    grouped = queries[0].reshape(own_count, KVH, group_size, HD)
    query_pos = hid_index * own_count + jnp.arange(own_count, dtype=jnp.int32)
    all_keys, all_values, span_keys, span_values = (
        lax.all_gather(cache_keys, "hid", axis=1, tiled=True),
        lax.all_gather(cache_values, "hid", axis=1, tiled=True),
        lax.all_gather(new_keys, "hid", axis=1, tiled=True),
        lax.all_gather(new_values, "hid", axis=1, tiled=True),
    )
    attn_state = empty_state(own_count)
    cache_len = all_keys.shape[1]
    step_size = block_size(cache_len)
    for offset in range(0, cache_len, step_size):
        attn_state = cache_block(
            attn_state,
            grouped,
            all_keys[0, offset : offset + step_size],
            all_values[0, offset : offset + step_size],
            offset,
            length,
        )
    span_len = span_keys.shape[1]
    step_size = block_size(span_len)
    offset = 0
    attn_state = span_block(
        attn_state,
        grouped,
        span_keys[0, offset : offset + step_size],
        span_values[0, offset : offset + step_size],
        offset,
        query_pos,
    )
    row_max, totals, accumulated = attn_state
    attended = (
        jnp.transpose(accumulated / totals[..., None], (2, 0, 1, 3))
        .reshape(own_count, QH * HD)
        .astype(jnp.bfloat16)
    )
    mid_stream = (
        hidden_in[0].astype(jnp.float32)
        + jnp.dot(attended, out_proj, preferred_element_type=jnp.float32)
    ).astype(jnp.bfloat16)
    moe_in = normalize(mid_stream, moe_gain).astype(jnp.bfloat16)
    logits = jnp.dot(moe_in, router, preferred_element_type=jnp.float32)
    expert_count = router.shape[1]
    top_count = routes.shape[2]
    capacity = 2 * own_count * top_count // expert_count
    pair_count = own_count * top_count
    all_routes = routes[0].reshape(hid_count, pair_count)
    onehot = (all_routes[..., None] == jnp.arange(expert_count, dtype=jnp.int32)).astype(jnp.int32)
    slot_ids = jnp.sum((jnp.cumsum(onehot, axis=1) - 1) * onehot, axis=-1)
    own_routes = lax.dynamic_index_in_dim(all_routes, hid_index, 0, keepdims=False)
    own_slots = lax.dynamic_index_in_dim(slot_ids, hid_index, 0, keepdims=False)
    own_targets = own_routes * capacity + own_slots
    pair_token = jnp.arange(pair_count, dtype=jnp.int32) // top_count
    picked = jnp.take_along_axis(logits, own_routes.reshape(own_count, top_count), axis=1)
    gate_values = jax.nn.sigmoid(picked)
    weights = gate_values / jnp.sum(gate_values, axis=1, keepdims=True)
    zero_row = jnp.zeros((1, model_width), jnp.bfloat16)
    all_rows = lax.all_gather(moe_in, "hid", axis=0, tiled=True)
    padded = jnp.concatenate([all_rows, zero_row], axis=0)
    source_ids = jnp.arange(hid_count, dtype=jnp.int32)[:, None] * own_count + pair_token[None, :]
    group_table = jnp.full((hid_count, expert_count * capacity), hid_count * own_count, jnp.int32)
    group_table = group_table.at[
        jnp.arange(hid_count, dtype=jnp.int32)[:, None], all_routes * capacity + slot_ids
    ].set(source_ids)
    send_rows = padded[group_table].reshape(hid_count, expert_count, capacity, model_width)
    grouped_rows = lax.all_to_all(send_rows, "req", split_axis=1, concat_axis=1, tiled=True)
    flat_rows = grouped_rows.reshape(-1, model_width)
    summed = lax.psum_scatter(
        jnp.dot(
            expert_activation(flat_rows, gate_up[0]),
            down_proj[0],
            preferred_element_type=jnp.float32,
        ).astype(jnp.bfloat16),
        "hid",
        scatter_dimension=0,
        tiled=True,
    )
    returned = lax.all_to_all(
        summed.reshape(-1, capacity, model_width), "req", split_axis=0, concat_axis=0, tiled=True
    )
    fetched = returned.reshape(expert_count * capacity, model_width)[own_targets].reshape(
        own_count, top_count, model_width
    )
    moe_out = jnp.sum(weights[..., None] * fetched.astype(jnp.float32), axis=1)
    final_rows = (mid_stream.astype(jnp.float32) + moe_out).astype(jnp.bfloat16)
    return (final_rows[None], new_keys, new_values)


def solution(mesh):
    in_specs = (
        P("req", "hid", None),
        P("req", "hid", None),
        P("req", "hid", None),
        P("req", "hid", None),
        P("req"),
        P("req", None, None),
        P(),
        P(),
        P(),
        P(),
        P(),
        P(),
        P("req", None, None, "hid"),
        P("req", "hid", None),
    )
    out_specs = (P("req", "hid", None), P("req", "hid", None), P("req", "hid", None))
    return jax.shard_map(body, mesh=mesh, in_specs=in_specs, out_specs=out_specs, check_vma=False)
```

profile of v0, /device:TPU:0, one launch (start us, length us, event | category | flops | bytes accessed | tf_op | source)
XLA Modules:
  0.0 660.1 jit_solution(17619439681119587326)
XLA Ops:
  7.3 2.2 copy.245
  9.6 2.0 copy.243
  14.4 7.6 %all-gather = bf16[512,256]{1,0:T(8,128)(2,1)} all-gather(bf16[128,256]{1,0:T(8,128)(2,1)S(1)} %convolution_convert_fusion.2), channel_id=2, replica_groups=mesh['req'=8,'hid'=4] {'hid'}, dimensions={0}, use_global_device_ids=true | all-gather | bytes 327680 | tf_op jit(solution)/shard_map/all_gather | solution.py:119
  22.3 8.1 %all-gather.1 = bf16[512,256]{1,0:T(8,128)(2,1)} all-gather(bf16[128,256]{1,0:T(8,128)(2,1)S(1)} %convolution_convert_fusion.1), channel_id=3, replica_groups=mesh['req'=8,'hid'=4] {'hid'}, dimensions={0}, use_global_device_ids=true | all-gather | bytes 327680 | tf_op jit(solution)/shard_map/all_gather | solution.py:120
  32.2 4.1 all-gather.8.cloned.1.call-done
  36.3 2.7 fusion.156
  39.0 21.5 %all-gather.6.cloned.1.call-done = bf16[1,4096,256]{1,2,0:T(8,128)(2,1)} async-done(((bf16[1,1024,256]{1,2,0:T(8,128)(2,1)}), bf16[1,4096,256]{1,2,0:T(8,128)(2,1)}) %all-gather.6.cloned.1.call-update) | async-done | bytes 2097168 | tf_op jit(solution)/shard_map/all_gather | solution.py:117
  60.5 1.6 fusion.157
  62.1 5.9 conditional.9
  63.5 1.6 fusion.18
  65.1 2.3 fusion.23
  68.1 5.3 conditional.10
  71.1 1.6 fusion.38
  73.3 5.2 conditional.11
  76.4 1.6 fusion.52
  78.6 5.5 conditional.12
  81.8 1.6 fusion.66
  84.1 5.2 conditional.13
  87.1 1.6 fusion.80
  89.3 5.2 conditional.14
  92.3 1.6 fusion.94
  94.6 5.6 conditional.15
  98.0 1.6 fusion.108
  100.2 7.2 %conditional.16 = ((f32[2,6,128]{2,1,0:T(8,128)}, f32[2,6,128]{2,1,0:T(8,128)S(1)}, f32[2,6,128,128]{3,2,1,0:T(8,128)S(1)})) conditional(s32[]{:T(128)} %convert_element_type.116, (f32[2,6,128]{2,1,0:T(8,128)}, f32[2,6,128]{2,1,0:T(8,128)S(1)}, f32[2,6,128,128]{3,2,1,0:T(8,128)S(1)}) %get-tuple-element.673, (s32[1,512]{1,0:T(1,128)S(1)}, ...), branch_computations={%region_28.0_spmd, %region_29.32_spmd} | conditional | flops 413274112 | bytes 13080608 | solution.py:47
  100.2 1.0 slice.47
  101.3 1.0 slice.46
  105.2 1.6 fusion.122
  107.5 4.5 conditional.17
  110.5 1.2 fusion.6
  112.1 3.2 multiply_reduce_fusion.1
  117.5 4.5 reduce-window.6
  122.8 8.1 %scatter_custom_fusion = s32[4096]{0:T(1024)S(1)} fusion(s32[2048]{0:T(1024)S(1)} %bitcast.353, s32[2048]{0:T(1024)S(1)} %bitcast.352, s32[]{:T(128)} %constant.115.clone.1), kind=kCustom, calls=%fused_computation.196 | custom fusion | bytes 16388
  130.9 3.4 all-gather.10.cloned.1.call-done
  134.3 1.5 concatenate.6
  135.8 19.2 %gather_fusion = bf16[4096,1536]{1,0:T(8,128)(2,1)} fusion(bf16[513,1536]{1,0:T(8,128)(2,1)S(1)} %concatenate.6, s32[4096]{0:T(1024)S(1)} %bitcast_clamp_fusion), kind=kCustom, calls=%fused_computation | custom fusion | bytes 25182208 | tf_op jit(solution)/shard_map/gather | solution.py:179
  155.1 6.6 copy.278
  161.6 278.6 %all_to_all.10 = bf16[4,8,128,1536]{3,2,0,1:T(8,128)(2,1)S(1)} all-to-all(bf16[4,8,128,1536]{3,2,0,1:T(8,128)(2,1)S(1)} %copy.278), channel_id=1, replica_groups=mesh['req'=8,'hid'=4] {'req'}, dimensions={1} | all-to-all | bytes 25165824 | tf_op jit(solution)/shard_map/all_to_all | solution.py:180
  440.2 1.9 copy.279
  442.2 4.5 copy-done.2
  446.6 6.0 convolution_maximum_fusion
  452.7 13.6 %convolution_convert_fusion = bf16[4096,1536]{1,0:T(8,128)(2,1)} fusion(f32[4096,192]{0,1:T(8,128)} %convolution_maximum_fusion, bf16[4096,1536]{1,0:T(8,128)(2,1)} %bitcast.316, bf16[1,192,1536]{2,1,0:T(8,128)(2,1)S(1)} %copy-done.8, bf16[1,2,1536,192]{2,3,1,0:T(8,128)(2,1)S(1)} %copy-done.5), kind=kOutput, calls=%fused_computation.152 | convolution fusion | flops 4839702528 | bytes 29491200 | tf_op jit(solution)/shard_map/dot_general | solution.py:183
  466.3 97.3 %reduce-scatter.2.cloned.1.call-done = bf16[1024,1536]{1,0:T(8,128)(2,1)} async-done(((bf16[4096,1536]{1,0:T(8,128)(2,1)}), bf16[1024,1536]{1,0:T(8,128)(2,1)}) %reduce-scatter.2.cloned.1.call-update) | async-done | bytes 3145744 | tf_op jit(solution)/shard_map/reduce_scatter | solution.py:182
  563.6 5.9 all-to-all-start.1
  571.2 2.6 gather_fusion.2
  574.2 66.1 %all-to-all-done.1 = bf16[8,128,1536]{2,1,0:T(8,128)(2,1)} async-done(((bf16[8,128,1536]{2,1,0:T(8,128)(2,1)}), bf16[8,128,1536]{2,1,0:T(8,128)(2,1)}, u32[]{:S(2)}, u32[]{:S(2)}) %all-to-all-start.1) | async-done | bytes 3145760 | tf_op jit(solution)/shard_map/all_to_all | solution.py:192
  640.2 5.9 gather_fusion.1
  646.2 2.2 reshape.354
  648.3 4.2 multiply_reduce_fusion
  (180 shorter events, 39.9 us)
Async XLA Ops:
  7.2 6.8 %copy-start = (bf16[1536,256]{1,0:T(8,128)(2,1)S(1)}, bf16[1536,256]{1,0:T(8,128)(2,1)}, u32[]{:S(2)}) copy-start(bf16[1536,256]{1,0:T(8,128)(2,1)} %param.39) | copy-start | bytes 2359300
  7.2 6.4 copy-start.9
  7.2 6.6 %copy-start.4 = (bf16[1,128,1536]{2,1,0:T(8,128)(2,1)S(1)}, bf16[1,128,1536]{2,1,0:T(8,128)(2,1)}, u32[]{:S(2)}) copy-start(bf16[1,128,1536]{2,1,0:T(8,128)(2,1)} %param.32) | copy-start | bytes 1179652
  7.2 6.8 %copy-start.29 = (f32[1536]{0:T(1024)S(1)}, f32[1536]{0:T(1024)}, u32[]{:S(2)}) copy-start(f32[1536]{0:T(1024)} %param.38) | copy-start | bytes 18436
  7.2 14.8 %copy-start.28 = (bf16[1536,256]{1,0:T(8,128)(2,1)S(1)}, bf16[1536,256]{1,0:T(8,128)(2,1)}, u32[]{:S(2)}) copy-start(bf16[1536,256]{1,0:T(8,128)(2,1)} %param.40) | copy-start | bytes 2359300
  7.2 29.1 %all-gather.8.cloned.1.call-start = ((), (), s32[]{:S(2)}) async-start(), calls=%async_computation.4 | async-start | bytes 2621440 | tf_op jit(solution)/shard_map/all_gather | solution.py:118
  9.5 51.0 %all-gather.6.cloned.1.call-start = ((), (), s32[]{:S(2)}) async-start(), calls=%async_computation.3 | async-start | bytes 2621440 | tf_op jit(solution)/shard_map/all_gather | solution.py:117
  11.6 122.7 %all-gather.10.cloned.1.call-start = ((), (), s32[]{:S(2)}) async-start(), calls=%async_computation.5 | async-start | bytes 1966080 | tf_op jit(solution)/shard_map/all_gather | solution.py:172
  14.3 47.8 %copy-start.16 = (bf16[128,256]{1,0:T(8,128)(2,1)}, bf16[128,256]{1,0:T(8,128)(2,1)S(1)}, u32[]{:S(2)}) copy-start(bf16[128,256]{1,0:T(8,128)(2,1)S(1)} %convolution_convert_fusion.2) | copy-start | bytes 196612
  22.3 39.8 %copy-start.17 = (bf16[128,256]{1,0:T(8,128)(2,1)}, bf16[128,256]{1,0:T(8,128)(2,1)S(1)}, u32[]{:S(2)}) copy-start(bf16[128,256]{1,0:T(8,128)(2,1)S(1)} %convolution_convert_fusion.1) | copy-start | bytes 196612
  62.1 5.9 copy-start.25
  68.0 5.3 copy-start.14
  68.0 5.3 copy-start.24
  68.1 3.0 copy-start.15
  73.3 5.3 copy-start.13
  73.3 5.3 copy-start.23
  78.6 5.5 copy-start.12
  78.6 5.5 copy-start.22
  84.1 5.3 copy-start.11
  84.1 5.3 copy-start.21
  89.3 5.2 copy-start.10
  100.2 7.3 %copy-start.6 = (bf16[512,256]{1,0:T(8,128)(2,1)S(1)}, bf16[512,256]{1,0:T(8,128)(2,1)}, u32[]{:S(2)}) copy-start(bf16[512,256]{1,0:T(8,128)(2,1)} %all-gather) | copy-start | bytes 786436
  100.2 7.3 %copy-start.7 = (bf16[512,256]{1,0:T(8,128)(2,1)S(1)}, bf16[512,256]{1,0:T(8,128)(2,1)}, u32[]{:S(2)}) copy-start(bf16[512,256]{1,0:T(8,128)(2,1)} %all-gather.1) | copy-start | bytes 786436
  112.1 3.3 copy-start.20
  112.1 4.4 copy-start.18
  115.4 7.3 %copy-start.27 = (s32[2]{0:T(128)S(1)}, s32[2]{0:T(128)}, u32[]{:S(2)}) copy-start(s32[2]{0:T(128)} %constant.193) | copy-start | bytes 28
  115.4 7.3 %copy-start.26 = (s32[2]{0:T(128)S(1)}, s32[2]{0:T(128)}, u32[]{:S(2)}) copy-start(s32[2]{0:T(128)} %constant.196) | copy-start | bytes 28
  116.3 447.3 %reduce-scatter.2.cloned.1.call-start = ((), (), s32[]{:S(2)}) async-start(), calls=%async_computation.6 | async-start | bytes 15728640 | tf_op jit(solution)/shard_map/reduce_scatter | solution.py:182
  440.2 6.4 copy-start.5
  442.2 4.5 copy-start.2
  446.6 6.0 copy-start.8
  563.6 7.4 %copy-start.3 = (bf16[128,1536]{1,0:T(8,128)(2,1)S(1)}, bf16[128,1536]{1,0:T(8,128)(2,1)}, u32[]{:S(2)}) copy-start(bf16[128,1536]{1,0:T(8,128)(2,1)} %multiply_convert_fusion) | copy-start | bytes 1179652
  563.6 7.5 %copy-start.19 = (bf16[1536,8]{0,1:T(8,128)(2,1)S(1)}, bf16[1536,8]{0,1:T(8,128)(2,1)}, u32[]{:S(2)}) copy-start(bf16[1536,8]{0,1:T(8,128)(2,1)} %param.43) | copy-start | bytes 73732
  563.6 76.7 %all-to-all-start.1 = ((bf16[8,128,1536]{2,1,0:T(8,128)(2,1)}), bf16[8,128,1536]{2,1,0:T(8,128)(2,1)}, u32[]{:S(2)}, u32[]{:S(2)}) async-start(bf16[8,128,1536]{2,1,0:T(8,128)(2,1)} %bitcast.327), calls=%async_computation.2 | async-start | bytes 6291456 | tf_op jit(solution)/shard_map/all_to_all | solution.py:192
  646.1 7.2 %copy-start.1 = (bf16[1536,256]{1,0:T(8,128)(2,1)S(1)}, bf16[1536,256]{1,0:T(8,128)(2,1)}, u32[]{:S(2)}) copy-start(bf16[1536,256]{1,0:T(8,128)(2,1)} %param.39) | copy-start | bytes 2359300
Sparse Core Ops, SparseCore 0:
  9.6 26.6 all-gather.7
  37.9 22.5 all-gather.5
  116.4 17.8 all-gather.9
  466.4 97.1 reduce-scatter.1
where the time goes:
time: 671 us; the launch traced here: 660 us
  blocking collectives  294 us (44%)
  waiting for transfers between devices  192 us (29%)
  local copies, waits for them, and re-layouts  71.4 us (11%)
  matrix products  44.6 us (7%)
  other arithmetic  34.3 us (5%)
  between operations  15.9 us (2%)
    all_to_all x1, blocking collectives, body(): lax.all_to_all(send_rows, 'req', split_axis=1, concat_axis=1, tiled=True)  279 us
    reduce_scatter x1, waiting for transfers between devices, body(): lax.psum_scatter(jnp.dot(expert_activation(flat_rows, gate_up[0]), down_p...  97.3 us
    all_to_all x1, waiting for transfers between devices, body(): lax.all_to_all(summed.reshape(-1, capacity, model_width), 'req', split_ax...  66.1 us
    all_gather x1, waiting for transfers between devices, body(): lax.all_gather(cache_keys, 'hid', axis=1, tiled=True)  21.5 us
    gather x1, local copies, waits for them, and re-layouts, body(): padded[group_table].reshape(hid_count, expert_count, capacity, model_width)  19.2 us
    unnamed x65, local copies, waits for them, and re-layouts  17.3 us
    dot_general x9, matrix products, absorb(): jnp.einsum('gstk,kgd->gstd', weights.astype(jnp.bfloat16), value_rows.res...  14.8 us
    dot_general x1, matrix products, body(): jnp.dot(expert_activation(flat_rows, gate_up[0]), down_proj[0], preferred...  13.6 us
  transfers between devices with their start and end apart: 5, of which 5 were waited for; matrix products, arithmetic and copies ran while one was open for 4% of the time, Pallas kernels for 0%

commit v1 on v0

v1 whole, which is shorter than its diff:
```python
import functools

import jax
import jax.numpy as jnp
from jax import lax
from jax.experimental import pallas as pl
from jax.experimental.pallas import tpu as pltpu
from jax.sharding import PartitionSpec as P

QH = 12
KVH = 2
HD = 128
GROUP = QH // KVH
EPS = 1e-06
MASKED_SCORE = -1e30
EXP2_SCALE = HD ** (-0.5) * 1.4426950408889634
ROW_TILE = 256
MESH = pl.DeviceIdType.MESH


def normalize(row_data, gain_vector):
    row_data = row_data.astype(jnp.float32)
    return (
        row_data
        * lax.rsqrt(jnp.mean(row_data * row_data, axis=-1, keepdims=True) + EPS)
        * gain_vector
    )


def dot_nt(left, right):
    return lax.dot_general(
        left, right, (((1,), (1,)), ((), ())), preferred_element_type=jnp.float32
    )


def layer_kernel(
    steps,
    hidden,
    queries,
    cache_keys,
    cache_values,
    lengths,
    routes_t,
    attn_gain,
    key_proj,
    value_proj,
    out_proj,
    moe_gain,
    router_t,
    gate_up,
    down_proj,
    layer_out,
    new_keys,
    new_values,
    kv,
    heads,
    acc,
    row_max,
    attended,
    out_w,
    mid,
    gate_in,
    gates,
    downs,
    act,
    toks,
    wts,
    parts,
    part_in,
    sum_in,
    local_sem,
    hid_send,
    hid_recv,
    req_send,
    req_recv,
):
    own = hidden.shape[0]
    half = cache_keys.shape[0] // 2
    span_slot = kv.shape[0] - 1
    width = gate_up.shape[2]
    experts = router_t.shape[0]
    me = lax.axis_index("hid")
    pair = me + 1 - 2 * lax.rem(me, 2)
    across = lax.rem(me + 2, 4)
    corner = 3 - me
    row = lax.axis_index("req")
    line, side = row // 2, lax.rem(row, 2)
    twin = {"req": line * 2 + 1 - side}

    def along(step):
        return {"req": lax.rem(line + step, steps) * 2 + side}

    barrier = pltpu.get_barrier_semaphore()
    for peer in [{"hid": pair}, {"hid": across}, twin] + [along(d) for d in range(1, steps)]:
        pl.semaphore_signal(barrier, inc=1, device_id=peer, device_id_type=MESH)
    pl.semaphore_wait(barrier, steps + 2)

    def hid_copy(src, dst, number, peer):
        return pltpu.make_async_remote_copy(
            src_ref=src,
            dst_ref=dst,
            send_sem=hid_send.at[number],
            recv_sem=hid_recv.at[number],
            device_id={"hid": peer},
            device_id_type=MESH,
        )

    def req_copy(src, dst, kind, slot, peer):
        return pltpu.make_async_remote_copy(
            src_ref=src,
            dst_ref=dst,
            send_sem=req_send.at[kind, slot],
            recv_sem=req_recv.at[kind, slot],
            device_id=peer,
            device_id_type=MESH,
        )

    cached = [
        (ref.at[pl.ds(part * half, half)], part, which)
        for part in range(2)
        for which, ref in enumerate((cache_keys, cache_values))
    ]
    for n, (src, part, which) in enumerate(cached):
        hid_copy(src, kv.at[me * 2 + part, which], n, across).start()
    for n, (src, part, which) in enumerate(cached):
        hid_copy(src, kv.at[me * 2 + part, which], 4 + n, pair).start()

    def own_block(n):
        src, part, which = cached[n]
        return pltpu.make_async_copy(src, kv.at[me * 2 + part, which], local_sem.at[n])

    for n in range(4):
        own_block(n).start()
    gate_load = pltpu.make_async_copy(gate_up, gate_in, local_sem.at[4])
    gate_load.start()
    down_load = pltpu.make_async_copy(down_proj, downs.at[me], local_sem.at[5])
    down_load.start()
    out_load = pltpu.make_async_copy(out_proj, out_w, local_sem.at[6])
    out_load.start()

    normed = normalize(hidden[...], attn_gain[...]).astype(jnp.bfloat16)
    own_rows = pl.ds(pl.multiple_of(me * own, own), own)
    for which, (proj, dest) in enumerate(((key_proj, new_keys), (value_proj, new_values))):
        fresh = jnp.dot(normed, proj[...], preferred_element_type=jnp.float32).astype(jnp.bfloat16)
        dest[...] = fresh
        kv[span_slot, which, own_rows, :] = fresh

    def span_rows(which, owner):
        return kv.at[span_slot, which, pl.ds(pl.multiple_of(owner * own, own), own)]

    for which in range(2):
        hid_copy(span_rows(which, me), span_rows(which, me), 12 + which, across).start()
        hid_copy(span_rows(which, me), span_rows(which, me), 14 + which, pair).start()

    for g in range(KVH):
        for i in range(GROUP):
            heads[g, i * own : (i + 1) * own, :] = queries[
                :, (g * GROUP + i) * HD : (g * GROUP + i + 1) * HD
            ]
    acc[...] = jnp.zeros_like(acc)
    row_max[...] = jnp.full_like(row_max, MASKED_SCORE)

    gate_load.wait()
    gates[me, :, 0:width] = gate_in[0]
    gates[me, :, width : 2 * width] = gate_in[1]
    hid_copy(gates.at[me], gates.at[me], 20, pair).start()
    hid_copy(down_proj, downs.at[me], 21, pair).start()

    def landed(dst, number):
        hid_copy(dst, dst, number, pair).wait_recv()

    length = lengths[0]
    ones = jnp.ones((half, HD), jnp.bfloat16)

    def step_body(step, carry):
        for n in range(2):

            @pl.when(step == n)
            def _():
                own_block(2 * n).wait()
                own_block(2 * n + 1).wait()

            @pl.when(step == 2 + n)
            def _():
                for which in range(2):
                    landed(kv.at[pair * 2 + n, which], 4 + 2 * n + which)

            @pl.when(step == 5 + 2 * n)
            def _():
                for which in range(2):
                    block = kv.at[across * 2 + n, which]
                    landed(block, 2 * n + which)
                    hid_copy(block, block, 8 + 2 * n + which, pair).start()
                if n == 1:
                    hid_copy(gates.at[me], gates.at[me], 18, across).start()
                    hid_copy(down_proj, downs.at[me], 19, across).start()

            @pl.when(step == 6 + 2 * n)
            def _():
                for which in range(2):
                    landed(kv.at[corner * 2 + n, which], 8 + 2 * n + which)

        @pl.when(step == 4)
        def _():
            for which in range(2):
                block = span_rows(which, across)
                landed(block, 12 + which)
                hid_copy(block, block, 16 + which, pair).start()
            for which in range(2):
                landed(span_rows(which, pair), 14 + which)
                landed(span_rows(which, corner), 16 + which)

        late = (step + 3) // 8
        span = (step + 4) // 8 - late
        early = 1 - span - late
        slot = (
            early * (2 * (me + (step // 2) * (pair - me)) + lax.rem(step, 2))
            + span * span_slot
            + late * (2 * (across + lax.rem(step + 1, 2) * (corner - across)) + (step + 1) // 2 - 3)
        )
        token = lax.broadcasted_iota(jnp.int32, (ROW_TILE, half), 0) % own
        column = lax.broadcasted_iota(jnp.int32, (ROW_TILE, half), 1)
        limit = (1 - span) * (length - slot * half) + span * (me * own + 1)
        visible = column < limit + span * token
        for g in range(KVH):
            keys = kv[slot, 0, :, g * HD : (g + 1) * HD]
            values = jnp.concatenate([kv[slot, 1, :, g * HD : (g + 1) * HD], ones], axis=1)
            for tile in range(GROUP * own // ROW_TILE):
                rows = slice(tile * ROW_TILE, (tile + 1) * ROW_TILE)
                scores = jnp.where(visible, dot_nt(heads[g, rows, :], keys), MASKED_SCORE)
                old_max = row_max[g, rows, :]
                new_max = jnp.maximum(old_max, jnp.max(scores, axis=1, keepdims=True))
                row_max[g, rows, :] = new_max
                rescale = jnp.exp2((old_max - new_max) * EXP2_SCALE)
                shift = jnp.concatenate([new_max] * (half // HD), axis=1)
                probs = jnp.exp2((scores - shift) * EXP2_SCALE).astype(jnp.bfloat16)
                acc[g, rows, :] = acc[g, rows, :] * jnp.concatenate([rescale, rescale], axis=1) + (
                    jnp.dot(probs, values, preferred_element_type=jnp.float32)
                )
        return carry

    lax.fori_loop(0, 9, step_body, 0)

    for g in range(KVH):
        for i in range(GROUP):
            rows = slice(i * own, (i + 1) * own)
            head = g * GROUP + i
            attended[:, head * HD : (head + 1) * HD] = (
                acc[g, rows, 0:HD] / acc[g, rows, HD : 2 * HD]
            ).astype(jnp.bfloat16)
    out_load.wait()
    cols = 512
    model = hidden.shape[1]
    for c in range(model // cols):
        at = slice(c * cols, (c + 1) * cols)
        mid[:, at] = (
            hidden[:, at].astype(jnp.float32)
            + jnp.dot(attended[...], out_w[:, at], preferred_element_type=jnp.float32)
        ).astype(jnp.bfloat16)

    moe_in = normalize(mid[...], moe_gain[...]).astype(jnp.bfloat16)
    toks[line, side] = moe_in
    logits = dot_nt(router_t[...], moe_in)
    own_routes = routes_t[:, own_rows]
    expert_ids = lax.broadcasted_iota(jnp.int32, (experts, own), 0)
    chosen = expert_ids == own_routes[0:1, :]
    for k in range(1, own_routes.shape[0]):
        chosen = chosen | (expert_ids == own_routes[k : k + 1, :])
    gate_values = jnp.where(chosen, jax.nn.sigmoid(logits), 0.0)
    weights = gate_values / jnp.sum(gate_values, axis=0, keepdims=True)
    high = weights.astype(jnp.bfloat16).astype(jnp.float32)
    wts[line, side] = jnp.concatenate([high, weights - high], axis=0).astype(jnp.bfloat16)

    def at_step(d):
        return lax.rem(line + steps - d, steps)

    for n, ref in enumerate((toks, wts)):
        req_copy(ref.at[line, side], ref.at[line, side], n, 0, twin).start()
        for d in range(1, steps):
            req_copy(ref.at[line, side], ref.at[line, side], 2 + n, d, along(d)).start()

    def pass_on(d, carry):
        for n, ref in enumerate((toks, wts)):
            block = ref.at[at_step(d), side]
            req_copy(block, block, 2 + n, d, twin).wait_recv()
            req_copy(block, block, n, d, twin).start()
        return carry

    lax.fori_loop(1, steps, pass_on, 0)

    down_load.wait()
    for n, ref in enumerate((gates, downs)):
        landed(ref.at[across], 18 + n)
        hid_copy(ref.at[across], ref.at[across], 22 + n, pair).start()
    for n, ref in enumerate((gates, downs)):
        landed(ref.at[pair], 20 + n)
        landed(ref.at[corner], 22 + n)

    pick = (lax.broadcasted_iota(jnp.int32, (2 * experts, HD), 0) % experts == row).astype(
        jnp.bfloat16
    )

    def expert_step(e, carry):
        d = lax.rem(e + 1, steps)
        source = at_step(d)
        for n, ref in enumerate((toks, wts)):
            block = ref.at[source, 1 - side]
            req_copy(block, block, n, d, twin).wait_recv()
        rows = toks[source].reshape(2 * own, model)
        for h in range(4):
            both = jnp.dot(rows, gates[h], preferred_element_type=jnp.float32)
            act[:, h * width : (h + 1) * width] = (
                jnp.maximum(both[:, 0:width], 0.0) * both[:, width : 2 * width]
            ).astype(jnp.bfloat16)
        share = jnp.concatenate(
            [
                lax.dot_general(
                    wts[source, s],
                    pick,
                    (((0,), (0,)), ((), ())),
                    preferred_element_type=jnp.float32,
                )
                for s in range(2)
            ],
            axis=0,
        )
        share = jnp.concatenate([share] * (cols // HD), axis=1)
        for c in range(model // cols):
            at = slice(c * cols, (c + 1) * cols)
            block = jnp.dot(
                act[...],
                downs[:, :, at].reshape(4 * width, cols),
                preferred_element_type=jnp.float32,
            )
            parts[d, :, :, at] = (block * share).astype(jnp.bfloat16).reshape(2, own, cols)
        req_copy(parts.at[d, 1 - side], part_in.at[d], 4, d, twin).start()

        @pl.when(e >= 1)
        def _():
            req_copy(part_in.at[e], part_in.at[e], 4, e, twin).wait_recv()
            parts[e, side] = (
                parts[e, side].astype(jnp.float32) + part_in[e].astype(jnp.float32)
            ).astype(jnp.bfloat16)
            req_copy(
                parts.at[e, side],
                sum_in.at[e - 1],
                5,
                e,
                {"req": at_step(e) * 2 + side},
            ).start()

        return carry

    lax.fori_loop(0, steps, expert_step, 0)

    total = mid[...].astype(jnp.float32) + parts[0, side].astype(jnp.float32)
    for d in range(1, steps):
        req_copy(sum_in.at[d - 1], sum_in.at[d - 1], 5, d, twin).wait_recv()
        total = total + sum_in[d - 1].astype(jnp.float32)
    req_copy(part_in.at[0], part_in.at[0], 4, 0, twin).wait_recv()
    layer_out[...] = (total + part_in[0].astype(jnp.float32)).astype(jnp.bfloat16)

    for n in range(12):
        src, part, which = cached[n % 4]
        hid_copy(src, kv.at[me * 2 + part, which], n, pair).wait_send()
    for n in range(12, 18):
        hid_copy(span_rows(0, me), span_rows(0, me), n, pair).wait_send()
    for n in range(18, 24):
        ref = (gates, downs)[n % 2]
        hid_copy(ref.at[me], ref.at[me], n, pair).wait_send()
    for n, ref in enumerate((toks, wts)):
        for d in range(steps):
            req_copy(ref.at[line, side], ref.at[line, side], n, d, twin).wait_send()
            if d:
                req_copy(ref.at[line, side], ref.at[line, side], 2 + n, d, twin).wait_send()
    for d in range(steps):
        req_copy(part_in.at[d], part_in.at[d], 4, d, twin).wait_send()
        if d:
            req_copy(parts.at[d, side], parts.at[d, side], 5, d, twin).wait_send()


def body(
    hidden_in,
    queries,
    cache_keys,
    cache_values,
    lengths,
    routes,
    attn_gain,
    key_proj,
    value_proj,
    out_proj,
    moe_gain,
    router,
    gate_up,
    down_proj,
):
    own, model = hidden_in.shape[1:]
    kv_width = key_proj.shape[1]
    cached = cache_keys.shape[1]
    steps = lax.axis_size("req") // 2
    experts = router.shape[1]
    width = gate_up.shape[3]
    bf16 = jnp.bfloat16
    vmem = pl.BlockSpec(memory_space=pltpu.VMEM)
    smem = pl.BlockSpec(memory_space=pltpu.SMEM)
    anywhere = pl.BlockSpec(memory_space=pl.ANY)
    layer_out, new_keys, new_values = pl.pallas_call(
        functools.partial(layer_kernel, steps),
        out_shape=(
            jax.ShapeDtypeStruct((own, model), bf16),
            jax.ShapeDtypeStruct((own, kv_width), bf16),
            jax.ShapeDtypeStruct((own, kv_width), bf16),
        ),
        in_specs=[
            vmem,
            vmem,
            anywhere,
            anywhere,
            smem,
            vmem,
            vmem,
            vmem,
            vmem,
            anywhere,
            vmem,
            vmem,
            anywhere,
            anywhere,
        ],
        out_specs=(vmem, vmem, vmem),
        scratch_shapes=[
            pltpu.VMEM((9, 2, cached // 2, kv_width), bf16),
            pltpu.VMEM((KVH, GROUP * own, HD), bf16),
            pltpu.VMEM((KVH, GROUP * own, 2 * HD), jnp.float32),
            pltpu.VMEM((KVH, GROUP * own, HD), jnp.float32),
            pltpu.VMEM((own, QH * HD), bf16),
            pltpu.VMEM(out_proj.shape, bf16),
            pltpu.VMEM((own, model), bf16),
            pltpu.VMEM((2, model, width), bf16),
            pltpu.VMEM((4, model, 2 * width), bf16),
            pltpu.VMEM((4, width, model), bf16),
            pltpu.VMEM((2 * own, 4 * width), bf16),
            pltpu.VMEM((steps, 2, own, model), bf16),
            pltpu.VMEM((steps, 2, 2 * experts, own), bf16),
            pltpu.VMEM((steps, 2, own, model), bf16),
            pltpu.VMEM((steps, own, model), bf16),
            pltpu.VMEM((steps - 1, own, model), bf16),
            pltpu.SemaphoreType.DMA((7,)),
            pltpu.SemaphoreType.DMA((24,)),
            pltpu.SemaphoreType.DMA((24,)),
            pltpu.SemaphoreType.DMA((6, steps)),
            pltpu.SemaphoreType.DMA((6, steps)),
        ],
        compiler_params=pltpu.CompilerParams(
            collective_id=0, has_side_effects=True, vmem_limit_bytes=VMEM_LIMIT
        ),
    )(
        hidden_in[0],
        queries[0],
        cache_keys[0],
        cache_values[0],
        lengths,
        routes[0].T,
        attn_gain[None],
        key_proj,
        value_proj,
        out_proj,
        moe_gain[None],
        router.T,
        gate_up[0],
        down_proj[0],
    )
    return (layer_out[None], new_keys[None], new_values[None])


VMEM_LIMIT = 64 * 1024 * 1024 - 512 * 1024


def solution(mesh):
    in_specs = (
        P("req", "hid", None),
        P("req", "hid", None),
        P("req", "hid", None),
        P("req", "hid", None),
        P("req"),
        P("req", None, None),
        P(),
        P(),
        P(),
        P(),
        P(),
        P(),
        P("req", None, None, "hid"),
        P("req", "hid", None),
    )
    out_specs = (P("req", "hid", None), P("req", "hid", None), P("req", "hid", None))
    return jax.shard_map(body, mesh=mesh, in_specs=in_specs, out_specs=out_specs, check_vma=False)
```

time: 671 us -> 156 us (0.23); the launches traced: 660 us -> 155 us
  blocking collectives: 294 us -> 0 us
  waiting for transfers between devices: 192 us -> 0 us
  Pallas kernels: 0 us -> 144 us
  local copies, waits for them, and re-layouts: 71.4 us -> 9.82 us
  matrix products: 44.6 us -> 0 us
  other arithmetic: 34.3 us -> 0 us
  between operations: 15.9 us -> 1.29 us
    all_to_all x1 -> x0, blocking collectives: 279 us -> none  [body(): lax.all_to_all(send_rows, 'req', split_axis=1, concat_axis=1, tiled=True)]
    pallas_call x0 -> x1, Pallas kernels: none -> 144 us  [body(): pl.pallas_call(functools.partial(layer_kernel, steps), out_shape=(jax.Sha...]
    reduce_scatter x1 -> x0, waiting for transfers between devices: 97.3 us -> none  [body(): lax.psum_scatter(jnp.dot(expert_activation(flat_rows, gate_up[0]), down_p...]
    all_to_all x1 -> x0, waiting for transfers between devices: 66.1 us -> none  [body(): lax.all_to_all(summed.reshape(-1, capacity, model_width), 'req', split_ax...]
    dot_general x24 -> x0, matrix products: 44.6 us -> none  [the longest x9 14.8 us: absorb(): jnp.einsum('gstk,kgd->gstd', weights.astype(jnp.bfloat16), value_rows.res...]
    all_gather x3 -> x0, waiting for transfers between devices: 29 us -> none  [the longest x1 21.5 us: body(): lax.all_gather(cache_keys, 'hid', axis=1, tiled=True)]
    gather x6 -> x0, local copies, waits for them, and re-layouts: 28 us -> none  [the longest x1 19.2 us: body(): padded[group_table].reshape(hid_count, expert_count, capacity, model_width)]
    all_gather x2 -> x0, blocking collectives: 15.7 us -> none  [the longest x1 8.1 us: body(): lax.all_gather(new_values, 'hid', axis=1, tiled=True)]
  transfers between devices with their start and end apart: 5 -> 0, of which waited for: 5 -> 0; matrix products, arithmetic and copies ran while one was open for 4% -> 0% of each run, Pallas kernels for 0% -> 0%
where the time goes in v1:
time: 156 us; the launch traced here: 155 us
  Pallas kernels  144 us (92%)
  local copies, waits for them, and re-layouts  9.82 us (6%)
    pallas_call x1, Pallas kernels, body(): pl.pallas_call(functools.partial(layer_kernel, steps), out_shape=(jax.Sha...  144 us
    unnamed x4, local copies, waits for them, and re-layouts  7.23 us

profile of v1, /device:TPU:0, one launch (start us, length us, event | category | flops | bytes accessed | tf_op | source)
XLA Modules:
  0.0 155.2 jit_solution(15063158266206518511)
XLA Ops:
  1.3 1.3 broadcast_in_dim.15.attn_gain
  2.6 1.3 broadcast_in_dim.16.moe_gain
  3.9 2.5 %copy.17 = bf16[1,2,1536,192]{3,2,1,0:T(8,128)(2,1)} copy(bf16[1,2,1536,192]{2,3,1,0:T(8,128)(2,1)} %param.26) | data formatting | bytes 2359296 | tf_op args[12]
  6.4 144.1 %shard_map.157 = (bf16[128,1536]{1,0:T(8,128)(2,1)}, bf16[128,256]{1,0:T(8,128)(2,1)}, bf16[128,256]{1,0:T(8,128)(2,1)}) custom-call(bf16[128,1536]{1,0:T(8,128)(2,1)} %bitcast.17, bf16[128,1536]{1,0:T(8,128)(2,1)} %bitcast.18, bf16[1024,256]{1,0:T(8,128)(2,1)} %bitcast.15, bf16[1024,256]{1,0:T(8,128)(2,1)} %bitcast.16, s32[1]{0:T(128)S(6)} %copy.21.lengths, ...), custom_call_target="tpu_custom_call" | custom-call | tf_op jit(solution)/shard_map/pallas_call | solution.py:408
  150.5 1.8 %copy.22 = bf16[1,128,1536]{2,1,0:T(8,128)(2,1)} copy(bf16[1,128,1536]{2,1,0:T(8,128)(2,1)} %bitcast.19) | data formatting | bytes 786432
  152.3 1.5 copy.23
  153.7 1.5 copy.24

commit v2 on v1

v2 whole, which is shorter than its diff:
```python
import functools

import jax
import jax.numpy as jnp
from jax import lax
from jax.experimental import pallas as pl
from jax.experimental.pallas import tpu as pltpu
from jax.sharding import PartitionSpec as P

QH = 12
KVH = 2
HD = 128
GROUP = QH // KVH
EPS = 1e-06
MASKED_SCORE = -1e30
EXP2_SCALE = HD ** (-0.5) * 1.4426950408889634
ROW_TILE = 256
MESH = pl.DeviceIdType.MESH


def normalize(row_data, gain_vector):
    row_data = row_data.astype(jnp.float32)
    return (
        row_data
        * lax.rsqrt(jnp.mean(row_data * row_data, axis=-1, keepdims=True) + EPS)
        * gain_vector
    )


def dot_nt(left, right):
    return lax.dot_general(
        left, right, (((1,), (1,)), ((), ())), preferred_element_type=jnp.float32
    )


def layer_kernel(
    steps,
    hidden,
    queries,
    cache_keys,
    cache_values,
    lengths,
    routes_t,
    attn_gain,
    key_proj,
    value_proj,
    out_proj,
    moe_gain,
    router_t,
    gate_up,
    down_proj,
    layer_out,
    new_keys,
    new_values,
    kv,
    heads,
    acc,
    row_max,
    attended,
    out_w,
    mid,
    gates,
    downs,
    act,
    toks,
    wts,
    parts,
    part_in,
    sum_in,
    local_sem,
    hid_send,
    hid_recv,
    req_send,
    req_recv,
):
    own = hidden.shape[0]
    half = cache_keys.shape[0] // 2
    span_slot = kv.shape[0] - 1
    width = down_proj.shape[0]
    experts = router_t.shape[0]
    me = lax.axis_index("hid")
    pair = me + 1 - 2 * lax.rem(me, 2)
    across = lax.rem(me + 2, 4)
    corner = 3 - me
    row = lax.axis_index("req")
    line, side = row // 2, lax.rem(row, 2)
    core, column_of = lax.rem(me, 2), me // 2
    own_slot, pair_slot = side * 2 + core, side * 2 + 1 - core
    far_slot, corner_slot = (1 - side) * 2 + core, (1 - side) * 2 + 1 - core
    neighbour = {"req": line * 2 + 1 - side}
    twin = {"hid": across}

    def along(place):
        return {"req": place * 2 + side}

    barrier = pltpu.get_barrier_semaphore()
    others = [along(lax.rem(line + d, steps)) for d in range(1, steps)]
    for peer in [{"hid": pair}, twin, neighbour] + others:
        pl.semaphore_signal(barrier, inc=1, device_id=peer, device_id_type=MESH)
    pl.semaphore_wait(barrier, steps + 2)

    def hid_copy(src, dst, number, peer):
        peer = peer if isinstance(peer, dict) else {"hid": peer}
        return pltpu.make_async_remote_copy(
            src_ref=src,
            dst_ref=dst,
            send_sem=hid_send.at[number],
            recv_sem=hid_recv.at[number],
            device_id=peer,
            device_id_type=MESH,
        )

    def req_copy(src, dst, kind, slot, peer, landing=None):
        return pltpu.make_async_remote_copy(
            src_ref=src,
            dst_ref=dst,
            send_sem=req_send.at[kind, slot],
            recv_sem=req_recv.at[kind, slot if landing is None else landing],
            device_id=peer,
            device_id_type=MESH,
        )

    cached = [
        (ref.at[pl.ds(part * half, half)], part, which)
        for part in range(2)
        for which, ref in enumerate((cache_keys, cache_values))
    ]
    for n, (src, part, which) in enumerate(cached[:2]):
        hid_copy(src, kv.at[me * 2 + part, which], n, across).start()
    for n, (src, part, which) in enumerate(cached):
        hid_copy(src, kv.at[me * 2 + part, which], 4 + n, pair).start()

    def own_block(n):
        src, part, which = cached[n]
        return pltpu.make_async_copy(src, kv.at[me * 2 + part, which], local_sem.at[n])

    for n in range(4):
        own_block(n).start()
    for n, peer in ((18, neighbour), (20, pair)):
        hid_copy(gate_up, gates.at[own_slot], n, peer).start()
        hid_copy(down_proj, downs.at[own_slot], n + 1, peer).start()
    gate_load = pltpu.make_async_copy(gate_up, gates.at[own_slot], local_sem.at[4])
    gate_load.start()
    down_load = pltpu.make_async_copy(down_proj, downs.at[own_slot], local_sem.at[5])
    down_load.start()
    out_load = pltpu.make_async_copy(out_proj, out_w, local_sem.at[6])
    out_load.start()

    normed = normalize(hidden[...], attn_gain[...]).astype(jnp.bfloat16)
    own_rows = pl.ds(pl.multiple_of(me * own, own), own)
    for which, (proj, dest) in enumerate(((key_proj, new_keys), (value_proj, new_values))):
        fresh = jnp.dot(normed, proj[...], preferred_element_type=jnp.float32).astype(jnp.bfloat16)
        dest[...] = fresh
        kv[span_slot, which, own_rows, :] = fresh

    def span_rows(which, owner):
        return kv.at[span_slot, which, pl.ds(pl.multiple_of(owner * own, own), own)]

    for which in range(2):
        hid_copy(span_rows(which, me), span_rows(which, me), 12 + which, across).start()
        hid_copy(span_rows(which, me), span_rows(which, me), 14 + which, pair).start()
    for n, (src, part, which) in enumerate(cached[2:]):
        hid_copy(src, kv.at[me * 2 + part, which], 2 + n, across).start()

    for g in range(KVH):
        for i in range(GROUP):
            heads[g, i * own : (i + 1) * own, :] = queries[
                :, (g * GROUP + i) * HD : (g * GROUP + i + 1) * HD
            ]
    acc[...] = jnp.zeros_like(acc)
    row_max[...] = jnp.full_like(row_max, MASKED_SCORE)

    def landed(dst, number):
        hid_copy(dst, dst, number, pair).wait_recv()

    length = lengths[0]
    ones = jnp.ones((half, HD), jnp.bfloat16)

    def absorb(slot, hide):
        for g in range(KVH):
            keys = kv[slot, 0, :, g * HD : (g + 1) * HD]
            values = jnp.concatenate([kv[slot, 1, :, g * HD : (g + 1) * HD], ones], axis=1)
            for tile in range(GROUP * own // ROW_TILE):
                rows = slice(tile * ROW_TILE, (tile + 1) * ROW_TILE)
                scores = hide(dot_nt(heads[g, rows, :], keys))
                old_max = row_max[g, rows, :]
                new_max = jnp.maximum(old_max, jnp.max(scores, axis=1, keepdims=True))
                row_max[g, rows, :] = new_max
                rescale = jnp.exp2((old_max - new_max) * EXP2_SCALE)
                shift = jnp.concatenate([new_max] * (half // HD), axis=1)
                probs = jnp.exp2((scores - shift) * EXP2_SCALE).astype(jnp.bfloat16)
                acc[g, rows, :] = acc[g, rows, :] * jnp.concatenate([rescale, rescale], axis=1) + (
                    jnp.dot(probs, values, preferred_element_type=jnp.float32)
                )

    def step_body(step, carry):
        for n in range(2):

            @pl.when(step == n)
            def _():
                own_block(2 * n).wait()
                own_block(2 * n + 1).wait()

            @pl.when(step == 2 + n)
            def _():
                for which in range(2):
                    landed(kv.at[pair * 2 + n, which], 4 + 2 * n + which)

            @pl.when(step == 4 + 3 * n)
            def _():
                for which in range(2):
                    block = kv.at[across * 2 + n, which]
                    landed(block, 2 * n + which)
                    hid_copy(block, block, 8 + 2 * n + which, pair).start()

            @pl.when(step == 5 + 3 * n)
            def _():
                for which in range(2):
                    landed(kv.at[corner * 2 + n, which], 8 + 2 * n + which)

        @pl.when(step == 6)
        def _():
            for which in range(2):
                block = span_rows(which, across)
                landed(block, 12 + which)
                hid_copy(block, block, 16 + which, pair).start()
            for which in range(2):
                landed(span_rows(which, pair), 14 + which)
                landed(span_rows(which, corner), 16 + which)

        early = 1 - (step + 4) // 8
        part = (step + 1) // 8
        span = (step + 2) // 8 - part
        late = 1 - early - span
        slot = (
            early * (2 * (me + (step // 2) * (pair - me)) + lax.rem(step, 2))
            + span * span_slot
            + late * (2 * (across + lax.rem(step + part, 2) * (corner - across)) + part)
        )

        @pl.when(step != 6)
        def _():
            column = lax.broadcasted_iota(jnp.int32, (1, half), 1)
            bias = jnp.where(column < length - slot * half, 0.0, MASKED_SCORE)
            absorb(slot, lambda scores: scores + bias)

        @pl.when(step == 6)
        def _():
            token = lax.broadcasted_iota(jnp.int32, (ROW_TILE, half), 0) % own
            column = lax.broadcasted_iota(jnp.int32, (ROW_TILE, half), 1)
            visible = column <= me * own + token
            absorb(span_slot, lambda scores: jnp.where(visible, scores, MASKED_SCORE))

        return carry

    lax.fori_loop(0, 9, step_body, 0)

    for g in range(KVH):
        for i in range(GROUP):
            rows = slice(i * own, (i + 1) * own)
            head = g * GROUP + i
            attended[:, head * HD : (head + 1) * HD] = (
                acc[g, rows, 0:HD] / acc[g, rows, HD : 2 * HD]
            ).astype(jnp.bfloat16)
    out_load.wait()
    cols = 512
    model = hidden.shape[1]
    for c in range(model // cols):
        at = slice(c * cols, (c + 1) * cols)
        mid[:, at] = (
            hidden[:, at].astype(jnp.float32)
            + jnp.dot(attended[...], out_w[:, at], preferred_element_type=jnp.float32)
        ).astype(jnp.bfloat16)

    moe_in = normalize(mid[...], moe_gain[...]).astype(jnp.bfloat16)
    toks[line, column_of] = moe_in
    logits = dot_nt(router_t[...], moe_in)
    own_routes = routes_t[:, own_rows]
    expert_ids = lax.broadcasted_iota(jnp.int32, (experts, own), 0)
    chosen = expert_ids == own_routes[0:1, :]
    for k in range(1, own_routes.shape[0]):
        chosen = chosen | (expert_ids == own_routes[k : k + 1, :])
    gate_values = jnp.where(chosen, jax.nn.sigmoid(logits), 0.0)
    weights = gate_values / jnp.sum(gate_values, axis=0, keepdims=True)
    high = weights.astype(jnp.bfloat16).astype(jnp.float32)
    wts[line, column_of] = jnp.concatenate([high, weights - high], axis=0).astype(jnp.bfloat16)

    def toks_copy(n, place, kind, peer, slot):
        block = (toks, wts)[n].at[place, column_of]
        return req_copy(block, block, 2 * kind + n, slot, peer)

    def give(place, up, down):
        for n in range(2):

            @pl.when(up)
            def _():
                toks_copy(n, place, 1, along(line + 1), place).start()

            @pl.when(down)
            def _():
                toks_copy(n, place, 2, along(line - 1), place).start()

            toks_copy(n, place, 0, twin, place).start()

    def schedule(t):
        dist = lax.rem(t // 2 + 1, steps)
        up = lax.rem(t, 2)
        place = line - dist + 2 * dist * up
        return place, up, (place >= 0) & (place < steps) & (t < 2 * steps - 1)

    def pass_on(t):
        place, up, valid = schedule(t)
        valid = valid & (t < 2 * steps - 2)
        for n in range(2):

            @pl.when(valid & (up == 0))
            def _():
                toks_copy(n, place, 1, twin, place).wait_recv()

                @pl.when(line + 1 < steps)
                def _():
                    toks_copy(n, place, 1, along(line + 1), place).start()

            @pl.when(valid & (up == 1))
            def _():
                toks_copy(n, place, 2, twin, place).wait_recv()

                @pl.when(line >= 1)
                def _():
                    toks_copy(n, place, 2, along(line - 1), place).start()

            @pl.when(valid)
            def _():
                toks_copy(n, place, 0, twin, place).start()

    give(line, line + 1 < steps, line >= 1)

    pass_on(0)
    pass_on(1)

    gate_load.wait()
    down_load.wait()
    for n, ref in enumerate((gates, downs)):
        landed(ref.at[far_slot], 18 + n)
        hid_copy(ref.at[far_slot], ref.at[far_slot], 22 + n, pair).start()
    for n, ref in enumerate((gates, downs)):
        landed(ref.at[pair_slot], 20 + n)
        landed(ref.at[corner_slot], 22 + n)

    lane_half = lax.broadcasted_iota(jnp.int32, (2 * experts, 2 * HD), 1) // HD
    pick = (
        lax.broadcasted_iota(jnp.int32, (2 * experts, 2 * HD), 0) % experts == line * 2 + lane_half
    ).astype(jnp.bfloat16)

    def expert_rows(place):
        for n, ref in enumerate((toks, wts)):
            block = ref.at[place, 1 - column_of]
            req_copy(block, block, n, place, twin).wait_recv()
        rows = toks[place].reshape(2 * own, model)
        share = jnp.concatenate(
            [
                lax.dot_general(
                    wts[place, s],
                    pick,
                    (((0,), (0,)), ((), ())),
                    preferred_element_type=jnp.float32,
                )
                for s in range(2)
            ],
            axis=0,
        )
        for h in range(4):
            both = dot_nt(rows, gates[h])
            one = share[:, (h // 2) * HD : (h // 2 + 1) * HD]
            scale = jnp.concatenate([one, one], axis=1)[:, 0:width]
            act[:, h * width : (h + 1) * width] = (
                jnp.maximum(both[:, 0:width], 0.0) * both[:, width : 2 * width] * scale
            ).astype(jnp.bfloat16)
        for c in range(model // cols):
            at = slice(c * cols, (c + 1) * cols)
            block = jnp.dot(
                act[...],
                downs[:, :, at].reshape(4 * width, cols),
                preferred_element_type=jnp.float32,
            )
            parts[place, :, :, at] = block.astype(jnp.bfloat16).reshape(2, own, cols)
        req_copy(parts.at[place, 1 - column_of], part_in.at[place], 6, place, twin).start()

    def send_back(place):
        req_copy(part_in.at[place], part_in.at[place], 6, place, twin).wait_recv()
        parts[place, column_of] = (
            parts[place, column_of].astype(jnp.float32) + part_in[place].astype(jnp.float32)
        ).astype(jnp.bfloat16)
        req_copy(
            parts.at[place, column_of], sum_in.at[line], 7, place, along(place), line
        ).start()

    def expert_step(t, carry):
        pass_on(t + 2)
        place, _, valid = schedule(t)

        @pl.when(valid)
        def _():
            expert_rows(place)

        past, _, was_valid = schedule(lax.rem(t + 2 * steps - 2, 2 * steps))

        @pl.when((t >= 2) & was_valid)
        def _():
            send_back(past)

        return carry

    lax.fori_loop(0, 2 * steps, expert_step, 0)

    req_copy(part_in.at[line], part_in.at[line], 6, line, twin).wait_recv()
    total = (
        mid[...].astype(jnp.float32)
        + parts[line, column_of].astype(jnp.float32)
        + part_in[line].astype(jnp.float32)
    )
    for d in range(1, steps):
        place = lax.rem(line + d, steps)
        req_copy(sum_in.at[place], sum_in.at[place], 7, place, twin).wait_recv()
        total = total + sum_in[place].astype(jnp.float32)
    layer_out[...] = total.astype(jnp.bfloat16)

    for n in range(12):
        src, part, which = cached[n % 4]
        hid_copy(src, kv.at[me * 2 + part, which], n, pair).wait_send()
    for n in range(12, 18):
        hid_copy(span_rows(0, me), span_rows(0, me), n, pair).wait_send()
    for n in range(18, 24):
        ref = (gates, downs)[n % 2]
        hid_copy(ref.at[own_slot], ref.at[own_slot], n, pair).wait_send()
    for place in range(steps):
        for n in range(2):
            toks_copy(n, place, 0, twin, place).wait_send()

            @pl.when((place <= line) & (line + 1 < steps))
            def _():
                toks_copy(n, place, 1, twin, place).wait_send()

            @pl.when((place >= line) & (line >= 1))
            def _():
                toks_copy(n, place, 2, twin, place).wait_send()

        req_copy(part_in.at[place], part_in.at[place], 6, place, twin).wait_send()

        @pl.when(place != line)
        def _():
            req_copy(part_in.at[place], part_in.at[place], 7, place, twin).wait_send()


def body(
    hidden_in,
    queries,
    cache_keys,
    cache_values,
    lengths,
    routes,
    attn_gain,
    key_proj,
    value_proj,
    out_proj,
    moe_gain,
    router,
    gate_up,
    down_proj,
):
    own, model = hidden_in.shape[1:]
    kv_width = key_proj.shape[1]
    cached = cache_keys.shape[1]
    steps = lax.axis_size("req") // 2
    experts = router.shape[1]
    width = gate_up.shape[3]
    bf16 = jnp.bfloat16
    vmem = pl.BlockSpec(memory_space=pltpu.VMEM)
    smem = pl.BlockSpec(memory_space=pltpu.SMEM)
    anywhere = pl.BlockSpec(memory_space=pl.ANY)
    layer_out, new_keys, new_values = pl.pallas_call(
        functools.partial(layer_kernel, steps),
        out_shape=(
            jax.ShapeDtypeStruct((own, model), bf16),
            jax.ShapeDtypeStruct((own, kv_width), bf16),
            jax.ShapeDtypeStruct((own, kv_width), bf16),
        ),
        in_specs=[
            vmem,
            vmem,
            anywhere,
            anywhere,
            smem,
            vmem,
            vmem,
            vmem,
            vmem,
            anywhere,
            vmem,
            vmem,
            anywhere,
            anywhere,
        ],
        out_specs=(vmem, vmem, vmem),
        scratch_shapes=[
            pltpu.VMEM((9, 2, cached // 2, kv_width), bf16),
            pltpu.VMEM((KVH, GROUP * own, HD), bf16),
            pltpu.VMEM((KVH, GROUP * own, 2 * HD), jnp.float32),
            pltpu.VMEM((KVH, GROUP * own, HD), jnp.float32),
            pltpu.VMEM((own, QH * HD), bf16),
            pltpu.VMEM(out_proj.shape, bf16),
            pltpu.VMEM((own, model), bf16),
            pltpu.VMEM((4, 2 * width, model), bf16),
            pltpu.VMEM((4, width, model), bf16),
            pltpu.VMEM((2 * own, 4 * width), bf16),
            pltpu.VMEM((steps, 2, own, model), bf16),
            pltpu.VMEM((steps, 2, 2 * experts, own), bf16),
            pltpu.VMEM((steps, 2, own, model), bf16),
            pltpu.VMEM((steps, own, model), bf16),
            pltpu.VMEM((steps, own, model), bf16),
            pltpu.SemaphoreType.DMA((7,)),
            pltpu.SemaphoreType.DMA((24,)),
            pltpu.SemaphoreType.DMA((24,)),
            pltpu.SemaphoreType.DMA((8, steps)),
            pltpu.SemaphoreType.DMA((8, steps)),
        ],
        compiler_params=pltpu.CompilerParams(
            collective_id=0, has_side_effects=True, vmem_limit_bytes=VMEM_LIMIT
        ),
    )(
        hidden_in[0],
        queries[0],
        cache_keys[0],
        cache_values[0],
        lengths,
        routes[0].T,
        attn_gain,
        key_proj,
        value_proj,
        out_proj,
        moe_gain,
        router.T,
        jnp.swapaxes(gate_up[0], 1, 2).reshape(2 * width, model),
        down_proj[0],
    )
    return (layer_out[None], new_keys[None], new_values[None])


VMEM_LIMIT = 64 * 1024 * 1024 - 512 * 1024


def solution(mesh):
    in_specs = (
        P("req", "hid", None),
        P("req", "hid", None),
        P("req", "hid", None),
        P("req", "hid", None),
        P("req"),
        P("req", None, None),
        P(),
        P(),
        P(),
        P(),
        P(),
        P(),
        P("req", None, None, "hid"),
        P("req", "hid", None),
    )
    out_specs = (P("req", "hid", None), P("req", "hid", None), P("req", "hid", None))
    return jax.shard_map(body, mesh=mesh, in_specs=in_specs, out_specs=out_specs, check_vma=False)
```

time: 156 us -> 132 us (0.85)
  the two profiles are of different devices: /device:TPU:0 before, /device:TPU:26 now
where the time goes in v2:
time: 132 us
  Pallas kernels  126 us (95%)
  local copies, waits for them, and re-layouts  4.71 us (4%)
    pallas_call x1, Pallas kernels, body(): pl.pallas_call(functools.partial(layer_kernel, steps), out_shape=(jax.Sha...  126 us
    unnamed x3, local copies, waits for them, and re-layouts  4.71 us

profile of v2, /device:TPU:26, one launch (start us, length us, event | category | flops | bytes accessed | tf_op | source)
XLA Modules:
  0.0 132.1 jit_solution(7808713886561755899)
XLA Ops:
  1.3 126.1 %shard_map.157 = (bf16[128,1536]{1,0:T(8,128)(2,1)}, bf16[128,256]{1,0:T(8,128)(2,1)}, bf16[128,256]{1,0:T(8,128)(2,1)}) custom-call(bf16[128,1536]{1,0:T(8,128)(2,1)} %bitcast.21, bf16[128,1536]{1,0:T(8,128)(2,1)} %bitcast.22, bf16[1024,256]{1,0:T(8,128)(2,1)} %bitcast.19, bf16[1024,256]{1,0:T(8,128)(2,1)} %bitcast.20, s32[1]{0:T(128)S(6)} %copy.20.lengths, ...), custom_call_target="tpu_custom_call" | custom-call | tf_op jit(solution)/shard_map/pallas_call | solution.py:481
  127.4 1.8 %copy.21 = bf16[1,128,1536]{2,1,0:T(8,128)(2,1)} copy(bf16[1,128,1536]{2,1,0:T(8,128)(2,1)} %bitcast.23) | data formatting | bytes 786432
  129.1 1.5 %copy.22 = bf16[1,128,256]{2,1,0:T(8,128)(2,1)} copy(bf16[1,128,256]{2,1,0:T(8,128)(2,1)} %bitcast.25) | data formatting | bytes 131072
  130.6 1.5 %copy.23 = bf16[1,128,256]{2,1,0:T(8,128)(2,1)} copy(bf16[1,128,256]{2,1,0:T(8,128)(2,1)} %bitcast.24) | data formatting | bytes 131072

commit v3 on v2

--- a/solution.py
+++ b/solution.py
@@ -174,12 +174,16 @@
         hid_copy(dst, dst, number, pair).wait_recv()
 
     length = lengths[0]
-    ones = jnp.ones((half, HD), jnp.bfloat16)
-
-    def absorb(slot, hide):
+
+    def absorb(slots, hide):
         for g in range(KVH):
-            keys = kv[slot, 0, :, g * HD : (g + 1) * HD]
-            values = jnp.concatenate([kv[slot, 1, :, g * HD : (g + 1) * HD], ones], axis=1)
+            keys = jnp.concatenate(
+                [kv[slot, 0, :, g * HD : (g + 1) * HD] for slot in slots], axis=0
+            )
+            values = jnp.concatenate(
+                [kv[slot, 1, :, g * HD : (g + 1) * HD] for slot in slots], axis=0
+            )
+            values = jnp.concatenate([values, jnp.ones_like(values)], axis=1)
             for tile in range(GROUP * own // ROW_TILE):
                 rows = slice(tile * ROW_TILE, (tile + 1) * ROW_TILE)
                 scores = hide(dot_nt(heads[g, rows, :], keys))
@@ -187,7 +191,7 @@
                 new_max = jnp.maximum(old_max, jnp.max(scores, axis=1, keepdims=True))
                 row_max[g, rows, :] = new_max
                 rescale = jnp.exp2((old_max - new_max) * EXP2_SCALE)
-                shift = jnp.concatenate([new_max] * (half // HD), axis=1)
+                shift = jnp.concatenate([new_max] * (len(slots) * half // HD), axis=1)
                 probs = jnp.exp2((scores - shift) * EXP2_SCALE).astype(jnp.bfloat16)
                 acc[g, rows, :] = acc[g, rows, :] * jnp.concatenate([rescale, rescale], axis=1) + (
                     jnp.dot(probs, values, preferred_element_type=jnp.float32)
@@ -196,29 +200,27 @@
     def step_body(step, carry):
         for n in range(2):
 
-            @pl.when(step == n)
+            @pl.when(step == 0)
             def _():
                 own_block(2 * n).wait()
                 own_block(2 * n + 1).wait()
 
-            @pl.when(step == 2 + n)
+            @pl.when(step == 1)
             def _():
                 for which in range(2):
                     landed(kv.at[pair * 2 + n, which], 4 + 2 * n + which)
 
-            @pl.when(step == 4 + 3 * n)
+            @pl.when(step == 2 + 2 * n)
             def _():
                 for which in range(2):
                     block = kv.at[across * 2 + n, which]
                     landed(block, 2 * n + which)
                     hid_copy(block, block, 8 + 2 * n + which, pair).start()
 
-            @pl.when(step == 5 + 3 * n)
-            def _():
                 for which in range(2):
                     landed(kv.at[corner * 2 + n, which], 8 + 2 * n + which)
 
-        @pl.when(step == 6)
+        @pl.when(step == 3)
         def _():
             for which in range(2):
                 block = span_rows(which, across)
@@ -228,32 +230,35 @@
                 landed(span_rows(which, pair), 14 + which)
                 landed(span_rows(which, corner), 16 + which)
 
-        early = 1 - (step + 4) // 8
-        part = (step + 1) // 8
-        span = (step + 2) // 8 - part
-        late = 1 - early - span
-        slot = (
-            early * (2 * (me + (step // 2) * (pair - me)) + lax.rem(step, 2))
-            + span * span_slot
-            + late * (2 * (across + lax.rem(step + part, 2) * (corner - across)) + part)
-        )
-
-        @pl.when(step != 6)
+        late = (step + 2) // 4
+        early = 1 - late
+        part = step // 4
+        source = me + lax.rem(step, 2) * (pair - me)
+        first = early * 2 * source + late * (2 * across + part)
+        second = early * (2 * source + 1) + late * (2 * corner + part)
+
+        @pl.when(step != 3)
         def _():
             column = lax.broadcasted_iota(jnp.int32, (1, half), 1)
-            bias = jnp.where(column < length - slot * half, 0.0, MASKED_SCORE)
-            absorb(slot, lambda scores: scores + bias)
-
-        @pl.when(step == 6)
+            bias = jnp.concatenate(
+                [
+                    jnp.where(column < length - slot * half, 0.0, MASKED_SCORE)
+                    for slot in (first, second)
+                ],
+                axis=1,
+            )
+            absorb((first, second), lambda scores: scores + bias)
+
+        @pl.when(step == 3)
         def _():
             token = lax.broadcasted_iota(jnp.int32, (ROW_TILE, half), 0) % own
             column = lax.broadcasted_iota(jnp.int32, (ROW_TILE, half), 1)
             visible = column <= me * own + token
-            absorb(span_slot, lambda scores: jnp.where(visible, scores, MASKED_SCORE))
+            absorb((span_slot,), lambda scores: jnp.where(visible, scores, MASKED_SCORE))
 
         return carry
 
-    lax.fori_loop(0, 9, step_body, 0)
+    lax.fori_loop(0, 5, step_body, 0)
 
     for g in range(KVH):
         for i in range(GROUP):

time: 132 us -> 134 us (1.015)
  the two profiles are of different devices: /device:TPU:26 before, /device:TPU:30 now
where the time goes in v3:
time: 134 us
  Pallas kernels  128 us (96%)
  local copies, waits for them, and re-layouts  4.71 us (4%)
    pallas_call x1, Pallas kernels, body(): pl.pallas_call(functools.partial(layer_kernel, steps), out_shape=(jax.Sha...  128 us
    unnamed x3, local copies, waits for them, and re-layouts  4.71 us

profile of v3, /device:TPU:30, one launch (start us, length us, event | category | flops | bytes accessed | tf_op | source)
XLA Modules:
  0.0 133.5 jit_solution(3313594763696566177)
XLA Ops:
  1.3 127.5 %shard_map.157 = (bf16[128,1536]{1,0:T(8,128)(2,1)}, bf16[128,256]{1,0:T(8,128)(2,1)}, bf16[128,256]{1,0:T(8,128)(2,1)}) custom-call(bf16[128,1536]{1,0:T(8,128)(2,1)} %bitcast.21, bf16[128,1536]{1,0:T(8,128)(2,1)} %bitcast.22, bf16[1024,256]{1,0:T(8,128)(2,1)} %bitcast.19, bf16[1024,256]{1,0:T(8,128)(2,1)} %bitcast.20, s32[1]{0:T(128)S(6)} %copy.20.lengths, ...), custom_call_target="tpu_custom_call" | custom-call | tf_op jit(solution)/shard_map/pallas_call | solution.py:486
  128.8 1.8 %copy.21 = bf16[1,128,1536]{2,1,0:T(8,128)(2,1)} copy(bf16[1,128,1536]{2,1,0:T(8,128)(2,1)} %bitcast.23) | data formatting | bytes 786432
  130.6 1.5 %copy.22 = bf16[1,128,256]{2,1,0:T(8,128)(2,1)} copy(bf16[1,128,256]{2,1,0:T(8,128)(2,1)} %bitcast.25) | data formatting | bytes 131072
  132.0 1.5 %copy.23 = bf16[1,128,256]{2,1,0:T(8,128)(2,1)} copy(bf16[1,128,256]{2,1,0:T(8,128)(2,1)} %bitcast.24) | data formatting | bytes 131072
